TPU v7x, 32 devices: a whole 2x2x4 slice. The times are simulated.
32 devices in a mesh: zslab: 4 (over y, x), blk: 8 (over z, core).
Axes of the slice: x: 2, y: 2, z: 4, core: 2. Of those that a mesh axis runs over, the one named last changes fastest.
Arguments:
- field: bfloat16 [64, 16, 16, 128], P('blk', None, 'zslab'), may hold values from -6 to 6
- fracture_mask: int32 [64, 16, 16], P('blk', None, 'zslab'), may hold values 0 or 1
- dilation: int32 [2, 3], replicated, may hold values from 1 to 2, as said below
- conv_weight: bfloat16 [2, 3456, 128], replicated, may hold values from -0.109375 to 0.109375
- embed_weight: bfloat16 [8, 2048, 1024], P('zslab', 'blk'), may hold values from -0.046875 to 0.046875
- qkv_weight: bfloat16 [3, 1024, 1024], P(None, 'blk', 'zslab'), may hold values from -3 to 3
- out_grad: bfloat16 [128, 1024], P('blk', 'zslab'), may hold values from -6 to 6
Outputs:
- field_grad: bfloat16 [64, 16, 16, 128], P('blk', None, 'zslab')
Inputs may be any that keep to these rules, and one draw needn't show every extreme that they name: The dilation of each of the 2 layers along x, y and z; some entry is 1 and some entry is 2.
All inputs are finite; a program needn't handle non-finite values. No bound on the sum of `fracture_mask` on one device may be relied on, other than what follows from the above.
Results may differ from a plain program's by a relative error of at most 0.04.
Values may be sent and summed in bfloat16 or wider, within the bound.
A program may use at most 64 MiB of HBM per device.

v0:
```python
import jax
import jax.numpy as jnp
from jax import lax
from jax.sharding import PartitionSpec as P

HD = 128
PY = 8
PZ = 2
LAYERS = 2
DMAX = 2


def padded_2(cells, sides, width):
    for axis, dim in sides:
        count = lax.axis_size(axis)
        ends = count - 1
        head = lax.slice_in_dim(cells, 0, width, axis=dim)
        tail = lax.slice_in_dim(cells, cells.shape[dim] - width, cells.shape[dim], axis=dim)
        cells = jnp.concatenate(
            [
                lax.ppermute(tail, axis, [(i, (i + 1) % count) for i in range(ends)]),
                cells,
                lax.ppermute(head, axis, [((i + 1) % count, i) for i in range(ends)]),
            ],
            axis=dim,
        )
    return cells


def with_rim(volume):
    padded = padded_2(volume, (("zslab", 2), ("blk", 0)), DMAX)
    return jnp.pad(padded, ((0, 0), (DMAX, DMAX), (0, 0), (0, 0)))


def apply_offsets(padded, weight, dilate, direction, dims_out):
    x_cells, y_cells, z_cells, channels = dims_out
    summed = jnp.zeros((x_cells * y_cells * z_cells, weight.shape[-1]), jnp.float32)
    for offset_x in (-1, 0, 1):
        pieces = []
        for offset_y in (-1, 0, 1):
            for offset_z in (-1, 0, 1):
                anchor = (
                    DMAX + direction * offset_x * dilate[0],
                    DMAX + direction * offset_y * dilate[1],
                    DMAX + direction * offset_z * dilate[2],
                    jnp.int32(0),
                )
                pieces.append(
                    lax.dynamic_slice(padded, anchor, (x_cells, y_cells, z_cells, channels))
                )
        stacked = jnp.concatenate(pieces, axis=3).reshape(x_cells * y_cells * z_cells, 9 * channels)
        group_rows = weight[(offset_x + 1) * 9 * channels : (offset_x + 2) * 9 * channels]
        summed = summed + jnp.dot(stacked, group_rows, preferred_element_type=jnp.float32)
    return summed.reshape(x_cells, y_cells, z_cells, -1)


def slab_total(term):
    return lax.psum(term.astype(jnp.bfloat16), "zslab").astype(jnp.float32)


def local(field, fracture_mask, dilation, conv_weight, embed_weight, qkv_weight, out_grad):
    x_cells, y_cells, z_cells, channels = field.shape
    gate_mask = fracture_mask.astype(jnp.float32)[..., None]
    hidden = field
    conv_outs = []
    for layer_num in range(LAYERS):
        conv_out = apply_offsets(
            with_rim(hidden), conv_weight[layer_num], dilation[layer_num], 1, field.shape
        )
        conv_outs.append(conv_out)
        hidden = (
            hidden.astype(jnp.float32) + gate_mask * (conv_out * jax.nn.sigmoid(conv_out))
        ).astype(jnp.bfloat16)
    slab_view = lax.all_to_all(hidden, "zslab", split_axis=0, concat_axis=2, tiled=True)
    x_local, z_total = (slab_view.shape[0], slab_view.shape[2])
    y_blocks, z_blocks = (y_cells // PY, z_total // PZ)
    patches = slab_view.reshape(x_local, y_blocks, PY, z_blocks, PZ, channels).transpose(
        1, 3, 0, 2, 4, 5
    )
    patches = patches.reshape(y_blocks * z_blocks, x_local, PY * PZ * channels)
    embed_rows, qkv_rows = (
        lax.all_gather(embed_weight, "blk", axis=1, tiled=True),
        lax.all_gather(qkv_weight, "blk", axis=1, tiled=True),
    )
    partial_value = jnp.einsum(
        "tpf,pfd->td", patches, embed_rows, preferred_element_type=jnp.float32
    )
    tokens = slab_total(partial_value).astype(jnp.bfloat16)
    projected = jnp.einsum(
        "td,sde->ste", tokens, qkv_rows, preferred_element_type=jnp.float32
    ).astype(jnp.bfloat16)
    key_rows, value_rows = (
        lax.all_gather(projected[1], "blk", axis=0, tiled=True),
        lax.all_gather(projected[2], "blk", axis=0, tiled=True),
    )
    tok_rows = tokens.shape[0]
    head_cols = projected.shape[2]
    heads_here = head_cols // HD
    inv_root = HD ** (-0.5)
    queries = projected[0].reshape(tok_rows, heads_here, HD)
    key_all = key_rows.reshape(-1, heads_here, HD)
    value_all = value_rows.reshape(-1, heads_here, HD)
    grad_out = out_grad.reshape(tok_rows, heads_here, HD)
    scores = (
        jnp.einsum("qhd,khd->hqk", queries, key_all, preferred_element_type=jnp.float32) * inv_root
    )
    top_score = jnp.max(scores, axis=2, keepdims=True)
    expo = jnp.exp(scores - top_score)
    total = jnp.sum(expo, axis=2, keepdims=True)
    probs = expo / total
    probs_b = probs.astype(jnp.bfloat16)
    attended = jnp.einsum("hqk,khd->qhd", probs_b, value_all, preferred_element_type=jnp.float32)
    row_delta = jnp.sum(grad_out.astype(jnp.float32) * attended, axis=2).T[:, :, None]
    score_grad = jnp.einsum("qhd,khd->hqk", grad_out, value_all, preferred_element_type=jnp.float32)
    dscore = (probs * (score_grad - row_delta) * inv_root).astype(jnp.bfloat16)
    grad_query = jnp.einsum("hqk,khd->qhd", dscore, key_all, preferred_element_type=jnp.float32)
    grad_query = grad_query.astype(jnp.bfloat16).reshape(tok_rows, head_cols)
    key_term = jnp.einsum("hqk,qhd->khd", dscore, queries, preferred_element_type=jnp.float32)
    value_term = jnp.einsum("hqk,qhd->khd", probs_b, grad_out, preferred_element_type=jnp.float32)
    key_value_grad = lax.psum_scatter(
        jnp.concatenate(
            [
                key_term.reshape(lax.axis_size("blk") * tok_rows, head_cols),
                value_term.reshape(lax.axis_size("blk") * tok_rows, head_cols),
            ],
            axis=1,
        ).astype(jnp.bfloat16),
        "blk",
        scatter_dimension=0,
        tiled=True,
    )
    grad_key = key_value_grad[:, :head_cols]
    grad_value = key_value_grad[:, head_cols:]
    stacked_grads = jnp.stack([grad_query, grad_key, grad_value])
    embed_rows, qkv_rows = (
        lax.all_gather(embed_weight, "blk", axis=1, tiled=True),
        lax.all_gather(qkv_weight, "blk", axis=1, tiled=True),
    )
    partial_grad = jnp.einsum(
        "ste,sde->td", stacked_grads, qkv_rows, preferred_element_type=jnp.float32
    )
    grad_tokens = slab_total(partial_grad).astype(jnp.bfloat16)
    patch_grad = jnp.einsum(
        "td,pfd->tpf", grad_tokens, embed_rows, preferred_element_type=jnp.float32
    ).astype(jnp.bfloat16)
    grid_grad = patch_grad.reshape(y_blocks, z_blocks, x_local, PY, PZ, channels).transpose(
        2, 0, 3, 1, 4, 5
    )
    grid_grad = grid_grad.reshape(x_local, y_cells, z_total, channels)
    grid_grad = lax.all_to_all(grid_grad, "zslab", split_axis=2, concat_axis=0, tiled=True)
    for layer_num in reversed(range(LAYERS)):
        conv_out = conv_outs[layer_num]
        sigma = jax.nn.sigmoid(conv_out)
        slope_grad = (
            gate_mask * sigma * (1.0 + conv_out * (1.0 - sigma)) * grid_grad.astype(jnp.float32)
        ).astype(jnp.bfloat16)
        flipped = (
            conv_weight[layer_num]
            .reshape(27, channels, channels)
            .transpose(0, 2, 1)
            .reshape(27 * channels, channels)
        )
        backward = apply_offsets(
            with_rim(slope_grad), flipped, dilation[layer_num], -1, field.shape
        )
        grid_grad = (grid_grad.astype(jnp.float32) + backward).astype(jnp.bfloat16)
    return grid_grad


def solution(mesh):
    return jax.shard_map(
        local,
        mesh=mesh,
        in_specs=(
            P("blk", None, "zslab", None),
            P("blk", None, "zslab"),
            P(),
            P(),
            P("zslab", "blk", None),
            P(None, "blk", "zslab"),
            P("blk", "zslab"),
        ),
        out_specs=P("blk", None, "zslab", None),
        check_vma=False,
    )
```

profile of v0, /device:TPU:1, one launch (start us, length us, event | category | flops | bytes accessed | tf_op | source)
XLA Modules:
  0.0 286.6 jit_solution(9424715995864858112)
XLA Ops:
  7.3 1.1 fusion.71
  8.4 3.9 %collective-permute-start = (bf16[8,16,2,128]{3,2,1,0:T(2,128)(2,1)S(1)}, bf16[8,16,2,128]{3,2,1,0:T(2,128)(2,1)S(1)}, u32[]{:S(2)}, u32[]{:S(2)}) collective-permute-start(bf16[8,16,2,128]{3,2,1,0:T(2,128)(2,1)S(1)} %get-tuple-element.133), channel_id=1, source_target_pairs={{0,8},{8,16},{16,24},{1,9},{9,17},{17,25},{2,10},{10,18},{18,26},{... | collective-permute-start | bytes 196616 | tf_op jit(solution)/shard_map/ppermute | solution.py:21
  12.4 1.3 collective-permute-start.1
  13.7 3.7 %collective-permute-done.1 = bf16[8,16,2,128]{3,2,1,0:T(2,128)(2,1)S(1)} collective-permute-done((bf16[8,16,2,128]{3,2,1,0:T(2,128)(2,1)S(1)}, bf16[8,16,2,128]{3,2,1,0:T(2,128)(2,1)S(1)}, u32[]{:S(2)}, u32[]{:S(2)}) %collective-permute-start.1) | collective-permute-done | bytes 65568 | tf_op jit(solution)/shard_map/ppermute | solution.py:23
  17.5 5.2 %collective-permute-start.2 = (bf16[2,16,8,128]{3,2,1,0:T(8,128)(2,1)S(1)}, bf16[2,16,8,128]{3,2,1,0:T(8,128)(2,1)S(1)}, u32[]{:S(2)}, u32[]{:S(2)}) collective-permute-start(bf16[2,16,8,128]{3,2,1,0:T(8,128)(2,1)S(1)} %get-tuple-element.125), channel_id=1, source_target_pairs={{0,1},{1,2},{2,3},{3,4},{4,5},{5,6},{6,7},{8,9},{9,10},{10,11},{11... | collective-permute-start | bytes 196616 | tf_op jit(solution)/shard_map/ppermute | solution.py:21
  22.7 1.9 collective-permute-start.3
  30.9 1.4 collective-permute-done.3
  35.5 1.0 copy-done.21
  36.5 1.0 copy-done.22
  37.6 2.4 reshape.172
  40.0 1.2 reshape.173
  41.1 3.3 %reshape.174 = bf16[512,1152]{1,0:T(8,128)(2,1)} reshape(bf16[8,16,4,1152]{3,2,1,0:T(4,128)(2,1)} %copy-done.21) | data formatting | bytes 2359296 | tf_op jit(solution)/shard_map/reshape | solution.py:51
  47.6 3.2 %collective-permute-start.4 = (bf16[8,16,2,128]{3,1,2,0:T(8,128)(2,1)S(1)}, bf16[8,16,2,128]{3,1,2,0:T(8,128)(2,1)S(1)}, u32[]{:S(2)}, u32[]{:S(2)}) collective-permute-start(bf16[8,16,2,128]{3,1,2,0:T(8,128)(2,1)S(1)} %get-tuple-element.131), channel_id=1, source_target_pairs={{0,8},{8,16},{16,24},{1,9},{9,17},{17,25},{2,10},{10,18},{18,26},{... | collective-permute-start | bytes 196616 | tf_op jit(solution)/shard_map/ppermute | solution.py:21
  50.9 1.3 collective-permute-start.5
  52.2 4.1 %collective-permute-done.5 = bf16[8,16,2,128]{3,1,2,0:T(8,128)(2,1)S(1)} collective-permute-done((bf16[8,16,2,128]{3,1,2,0:T(8,128)(2,1)S(1)}, bf16[8,16,2,128]{3,1,2,0:T(8,128)(2,1)S(1)}, u32[]{:S(2)}, u32[]{:S(2)}) %collective-permute-start.5) | collective-permute-done | bytes 65568 | tf_op jit(solution)/shard_map/ppermute | solution.py:23
  56.3 4.4 %collective-permute-start.6 = (bf16[2,16,8,128]{3,1,2,0:T(8,128)(2,1)S(1)}, bf16[2,16,8,128]{3,1,2,0:T(8,128)(2,1)S(1)}, u32[]{:S(2)}, u32[]{:S(2)}) collective-permute-start(bf16[2,16,8,128]{3,1,2,0:T(8,128)(2,1)S(1)} %get-tuple-element.123), channel_id=1, source_target_pairs={{0,1},{1,2},{2,3},{3,4},{4,5},{5,6},{6,7},{8,9},{9,10},{10,11},{11... | collective-permute-start | bytes 196616 | tf_op jit(solution)/shard_map/ppermute | solution.py:21
  60.7 1.9 collective-permute-start.7
  71.4 1.1 copy-done.18
  72.4 1.0 copy-done.23
  73.9 1.2 reshape.176
  75.1 1.8 copy.107
  76.9 1.2 reshape.177
  78.1 1.8 copy.108
  79.9 1.2 reshape.178
  81.0 1.8 fusion.27
  85.4 6.6 %all_to_all.24 = bf16[8,16,4,128]{3,1,2,0:T(8,128)(2,1)S(1)} all-to-all(bf16[8,16,4,128]{3,1,2,0:T(8,128)(2,1)S(1)} %add_convert_fusion), channel_id=1, replica_groups=mesh['zslab'=4,'blk'=8] {'zslab'}, dimensions={0} | all-to-all | bytes 262144 | tf_op jit(solution)/shard_map/all_to_all | solution.py:74
  92.2 2.7 all-gather.5.cloned.1.call-done
  94.9 4.6 %fusion.2 = bf16[16,1024]{1,0:T(8,128)(2,1)S(1)} fusion(bf16[16,2,2048]{2,0,1:T(8,128)(2,1)S(1)} %reshape.181, bf16[2,2048,1024]{2,1,0:T(8,128)(2,1)} %all-gather.5.cloned.1.call-done), kind=kOutput, calls=%fused_computation.19 | convolution fusion | flops 134234112 | bytes 8552448 | tf_op jit(solution)/shard_map/tpf,pfd->td/dot_general | solution.py:85
  99.5 13.7 %psum.14 = bf16[16,1024]{1,0:T(8,128)(2,1)S(1)} all-reduce(bf16[16,1024]{1,0:T(8,128)(2,1)S(1)} %fusion.2), channel_id=1, replica_groups=mesh['zslab'=4,'blk'=8] {'zslab'}, use_global_device_ids=true, to_apply=%region_0.1 | all-reduce | flops 16384 | bytes 65536 | tf_op jit(solution)/shard_map/psum | solution.py:58
  113.1 7.0 %all-gather.7.cloned.1.call-done = bf16[3,1024,256]{2,1,0:T(8,128)(2,1)} async-done(((bf16[3,128,256]{2,1,0:T(8,128)(2,1)}), bf16[3,1024,256]{2,1,0:T(8,128)(2,1)}) %all-gather.7.cloned.1.call-update) | async-done | bytes 1572880 | tf_op jit(solution)/shard_map/all_gather | solution.py:83
  120.1 1.7 fusion.4
  121.9 14.2 %all-gather = bf16[1,128,256]{2,1,0:T(8,128)(2,1)S(1)} all-gather(bf16[1,16,256]{2,1,0:T(8,128)(2,1)S(1)} %get-tuple-element.137), channel_id=2, replica_groups=mesh['zslab'=4,'blk'=8] {'blk'}, dimensions={1}, use_global_device_ids=true | all-gather | bytes 73728 | tf_op jit(solution)/shard_map/all_gather | solution.py:93
  136.6 14.0 %all-gather.1 = bf16[1,128,256]{2,1,0:T(8,128)(2,1)S(1)} all-gather(bf16[1,16,256]{2,1,0:T(8,128)(2,1)S(1)} %get-tuple-element.135), channel_id=3, replica_groups=mesh['zslab'=4,'blk'=8] {'blk'}, dimensions={1}, use_global_device_ids=true | all-gather | bytes 73728 | tf_op jit(solution)/shard_map/all_gather | solution.py:94
  152.1 1.1 fusion.12
  153.2 1.0 fusion.11
  155.2 0.9 copy.124
  156.1 1.5 pad_maximum_fusion
  157.8 25.7 %reduce-scatter.2.cloned.1.call-done = bf16[16,512]{1,0:T(8,128)(2,1)} async-done(((bf16[128,512]{1,0:T(8,128)(2,1)}), bf16[16,512]{1,0:T(8,128)(2,1)}) %reduce-scatter.2.cloned.1.call-update) | async-done | bytes 16400 | tf_op jit(solution)/shard_map/reduce_scatter | solution.py:120
  184.8 12.8 %psum.15 = bf16[16,1024]{1,0:T(8,128)(2,1)S(1)} all-reduce(bf16[16,1024]{1,0:T(8,128)(2,1)S(1)} %fusion.3), channel_id=1, replica_groups=mesh['zslab'=4,'blk'=8] {'zslab'}, use_global_device_ids=true, to_apply=%region_5.6 | all-reduce | flops 16384 | bytes 65536 | tf_op jit(solution)/shard_map/psum | solution.py:58
  197.6 5.7 %convolution_convert_fusion = bf16[16,2,2048]{2,0,1:T(8,128)(2,1)S(1)} fusion(bf16[2,2048,1024]{2,1,0:T(8,128)(2,1)} %all-gather.5.cloned.1.call-done, bf16[16,1024]{1,0:T(8,128)(2,1)S(1)} %psum.15), kind=kOutput, calls=%fused_computation.1 | convolution fusion | flops 134283264 | bytes 8552448 | tf_op jit(solution)/shard_map/td,pfd->tpf/dot_general | solution.py:143
  203.3 6.4 %all_to_all.25 = bf16[2,16,16,128]{3,1,0,2:T(8,128)(2,1)S(1)} all-to-all(bf16[2,16,16,128]{3,1,0,2:T(8,128)(2,1)S(1)} %copy.126), channel_id=1, replica_groups=mesh['zslab'=4,'blk'=8] {'zslab'}, dimensions={2} | all-to-all | bytes 262144 | tf_op jit(solution)/shard_map/all_to_all | solution.py:150
  210.0 2.5 collective-permute-start.8
  212.6 1.5 collective-permute-start.9
  214.1 1.0 fusion.65
  215.1 3.1 %collective-permute-done.9 = bf16[8,16,2,128]{3,1,2,0:T(8,128)(2,1)S(1)} collective-permute-done((bf16[8,16,2,128]{3,1,2,0:T(8,128)(2,1)S(1)}, bf16[8,16,2,128]{3,1,2,0:T(8,128)(2,1)S(1)}, u32[]{:S(2)}, u32[]{:S(2)}) %collective-permute-start.9) | collective-permute-done | bytes 65568 | tf_op jit(solution)/shard_map/ppermute | solution.py:23
  218.2 8.9 %collective-permute-start.10 = (bf16[2,16,8,128]{3,1,2,0:T(8,128)(2,1)S(1)}, bf16[2,16,8,128]{3,1,2,0:T(8,128)(2,1)S(1)}, u32[]{:S(2)}, u32[]{:S(2)}) collective-permute-start(bf16[2,16,8,128]{3,1,2,0:T(8,128)(2,1)S(1)} %get-tuple-element.121), channel_id=1, source_target_pairs={{0,1},{1,2},{2,3},{3,4},{4,5},{5,6},{6,7},{8,9},{9,10},{10,11},{11... | collective-permute-start | bytes 196616 | tf_op jit(solution)/shard_map/ppermute | solution.py:21
  227.1 3.8 %collective-permute-start.11 = (bf16[2,16,8,128]{3,1,2,0:T(8,128)(2,1)S(1)}, bf16[2,16,8,128]{3,1,2,0:T(8,128)(2,1)S(1)}, u32[]{:S(2)}, u32[]{:S(2)}) collective-permute-start(bf16[2,16,8,128]{3,1,2,0:T(8,128)(2,1)S(1)} %get-tuple-element.122), channel_id=1, source_target_pairs={{1,0},{2,1},{3,2},{4,3},{5,4},{6,5},{7,6},{9,8},{10,9},{11,10},{12... | collective-permute-start | bytes 196616 | tf_op jit(solution)/shard_map/ppermute | solution.py:23
  235.9 1.0 copy-done.19
  237.0 1.0 copy-done.24
  238.8 1.8 copy.132
  240.9 1.8 copy.134
  242.6 1.2 reshape.191
  243.8 1.5 fusion.75
  247.9 4.2 %collective-permute-start.12 = (bf16[8,16,2,128]{3,1,2,0:T(8,128)(2,1)S(1)}, bf16[8,16,2,128]{3,1,2,0:T(8,128)(2,1)S(1)}, u32[]{:S(2)}, u32[]{:S(2)}) collective-permute-start(bf16[8,16,2,128]{3,1,2,0:T(8,128)(2,1)S(1)} %get-tuple-element.127), channel_id=1, source_target_pairs={{0,8},{8,16},{16,24},{1,9},{9,17},{17,25},{2,10},{10,18},{18,26},{... | collective-permute-start | bytes 196616 | tf_op jit(solution)/shard_map/ppermute | solution.py:21
  252.1 1.3 collective-permute-start.13
  253.9 4.1 %collective-permute-done.13 = bf16[8,16,2,128]{3,1,2,0:T(8,128)(2,1)S(1)} collective-permute-done((bf16[8,16,2,128]{3,1,2,0:T(8,128)(2,1)S(1)}, bf16[8,16,2,128]{3,1,2,0:T(8,128)(2,1)S(1)}, u32[]{:S(2)}, u32[]{:S(2)}) %collective-permute-start.13) | collective-permute-done | bytes 65568 | tf_op jit(solution)/shard_map/ppermute | solution.py:23
  258.0 2.4 collective-permute-start.14
  260.4 2.2 collective-permute-start.15
  268.2 1.0 copy-done.20
  269.2 1.0 copy-done.25
  271.0 1.8 copy.140
  273.1 1.8 copy.142
  274.9 1.2 reshape.195
  276.1 1.5 fusion.76
  (184 shorter events, 36.9 us)
Async XLA Ops:
  6.5 144.7 %copy-start = (bf16[16,256]{1,0:T(8,128)(2,1)S(1)}, bf16[16,256]{1,0:T(8,128)(2,1)}, u32[]{:S(2)}) copy-start(bf16[16,256]{1,0:T(8,128)(2,1)} %param.13) | copy-start | bytes 24580
  6.5 10.9 %copy-start.11 = (bf16[8,16,4,128]{3,2,1,0:T(4,128)(2,1)S(1)}, bf16[8,16,4,128]{3,2,1,0:T(4,128)(2,1)}, u32[]{:S(2)}) copy-start(bf16[8,16,4,128]{3,2,1,0:T(4,128)(2,1)} %param.7) | copy-start | bytes 393220
  6.5 18.1 %copy-start.34 = (s32[2,3]{1,0:T(2,128)S(1)}, s32[2,3]{1,0:T(2,128)}, u32[]{:S(2)}) copy-start(s32[2,3]{1,0:T(2,128)} %param.9) | copy-start | bytes 76
  6.5 24.3 %copy-start.33 = (s32[8,16,4]{1,2,0:T(4,128)S(1)}, s32[8,16,4]{1,2,0:T(4,128)}, u32[]{:S(2)}) copy-start(s32[8,16,4]{1,2,0:T(4,128)} %param.8) | copy-start | bytes 6148
  6.5 88.3 %all-gather.5.cloned.1.call-start = ((), (), s32[]{:S(2)}) async-start(), calls=%async_computation.3 | async-start | bytes 9437184 | tf_op jit(solution)/shard_map/all_gather | solution.py:82
  7.3 112.9 %all-gather.7.cloned.1.call-start = ((), (), s32[]{:S(2)}) async-start(), calls=%async_computation.4 | async-start | bytes 1769472 | tf_op jit(solution)/shard_map/all_gather | solution.py:83
  8.4 5.3 %collective-permute-start = (bf16[8,16,2,128]{3,2,1,0:T(2,128)(2,1)S(1)}, bf16[8,16,2,128]{3,2,1,0:T(2,128)(2,1)S(1)}, u32[]{:S(2)}, u32[]{:S(2)}) collective-permute-start(bf16[8,16,2,128]{3,2,1,0:T(2,128)(2,1)S(1)} %get-tuple-element.133), channel_id=1, source_target_pairs={{0,8},{8,16},{16,24},{1,9},{9,17},{17,25},{2,10},{10,18},{18,26},{... | collective-permute-start | bytes 196616 | tf_op jit(solution)/shard_map/ppermute | solution.py:21
  12.4 5.0 %collective-permute-start.1 = (bf16[8,16,2,128]{3,2,1,0:T(2,128)(2,1)S(1)}, bf16[8,16,2,128]{3,2,1,0:T(2,128)(2,1)S(1)}, u32[]{:S(2)}, u32[]{:S(2)}) collective-permute-start(bf16[8,16,2,128]{3,2,1,0:T(2,128)(2,1)S(1)} %get-tuple-element.134), channel_id=1, source_target_pairs={{8,0},{16,8},{24,16},{9,1},{17,9},{25,17},{10,2},{18,10},{26,18},{... | collective-permute-start | bytes 196616 | tf_op jit(solution)/shard_map/ppermute | solution.py:23
  17.5 13.4 %collective-permute-start.2 = (bf16[2,16,8,128]{3,2,1,0:T(8,128)(2,1)S(1)}, bf16[2,16,8,128]{3,2,1,0:T(8,128)(2,1)S(1)}, u32[]{:S(2)}, u32[]{:S(2)}) collective-permute-start(bf16[2,16,8,128]{3,2,1,0:T(8,128)(2,1)S(1)} %get-tuple-element.125), channel_id=1, source_target_pairs={{0,1},{1,2},{2,3},{3,4},{4,5},{5,6},{6,7},{8,9},{9,10},{10,11},{11... | collective-permute-start | bytes 196616 | tf_op jit(solution)/shard_map/ppermute | solution.py:21
  22.7 9.5 %collective-permute-start.3 = (bf16[2,16,8,128]{3,2,1,0:T(8,128)(2,1)S(1)}, bf16[2,16,8,128]{3,2,1,0:T(8,128)(2,1)S(1)}, u32[]{:S(2)}, u32[]{:S(2)}) collective-permute-start(bf16[2,16,8,128]{3,2,1,0:T(8,128)(2,1)S(1)} %get-tuple-element.126), channel_id=1, source_target_pairs={{1,0},{2,1},{3,2},{4,3},{5,4},{6,5},{7,6},{9,8},{10,9},{11,10},{12... | collective-permute-start | bytes 196616 | tf_op jit(solution)/shard_map/ppermute | solution.py:23
  30.8 179.0 %copy-start.31 = (f32[8,16,4]{1,2,0:T(4,128)}, f32[8,16,4]{1,2,0:T(4,128)S(1)}, u32[]{:S(2)}) copy-start(f32[8,16,4]{1,2,0:T(4,128)S(1)} %convert_element_type.85) | copy-start | bytes 6148
  35.5 1.1 copy-start.21
  36.5 1.0 copy-start.22
  41.1 3.3 %copy-start.2 = (bf16[2,3456,128]{2,1,0:T(8,128)(2,1)S(1)}, bf16[2,3456,128]{2,1,0:T(8,128)(2,1)}, u32[]{:S(2)}) copy-start(bf16[2,3456,128]{2,1,0:T(8,128)(2,1)} %param.10) | copy-start | bytes 5308420
  44.4 1.3 copy-start.7
  45.7 1.3 copy-start.8
  47.4 22.0 %copy-start.12 = (f32[512,128]{1,0:T(8,128)}, f32[512,128]{1,0:T(8,128)S(1)}, u32[]{:S(2)}) copy-start(f32[512,128]{1,0:T(8,128)S(1)} %convolution_add_fusion.6) | copy-start | bytes 786436
  47.6 4.6 %collective-permute-start.4 = (bf16[8,16,2,128]{3,1,2,0:T(8,128)(2,1)S(1)}, bf16[8,16,2,128]{3,1,2,0:T(8,128)(2,1)S(1)}, u32[]{:S(2)}, u32[]{:S(2)}) collective-permute-start(bf16[8,16,2,128]{3,1,2,0:T(8,128)(2,1)S(1)} %get-tuple-element.131), channel_id=1, source_target_pairs={{0,8},{8,16},{16,24},{1,9},{9,17},{17,25},{2,10},{10,18},{18,26},{... | collective-permute-start | bytes 196616 | tf_op jit(solution)/shard_map/ppermute | solution.py:21
  50.9 5.4 %collective-permute-start.5 = (bf16[8,16,2,128]{3,1,2,0:T(8,128)(2,1)S(1)}, bf16[8,16,2,128]{3,1,2,0:T(8,128)(2,1)S(1)}, u32[]{:S(2)}, u32[]{:S(2)}) collective-permute-start(bf16[8,16,2,128]{3,1,2,0:T(8,128)(2,1)S(1)} %get-tuple-element.132), channel_id=1, source_target_pairs={{8,0},{16,8},{24,16},{9,1},{17,9},{25,17},{10,2},{18,10},{26,18},{... | collective-permute-start | bytes 196616 | tf_op jit(solution)/shard_map/ppermute | solution.py:23
  56.3 12.1 %collective-permute-start.6 = (bf16[2,16,8,128]{3,1,2,0:T(8,128)(2,1)S(1)}, bf16[2,16,8,128]{3,1,2,0:T(8,128)(2,1)S(1)}, u32[]{:S(2)}, u32[]{:S(2)}) collective-permute-start(bf16[2,16,8,128]{3,1,2,0:T(8,128)(2,1)S(1)} %get-tuple-element.123), channel_id=1, source_target_pairs={{0,1},{1,2},{2,3},{3,4},{4,5},{5,6},{6,7},{8,9},{9,10},{10,11},{11... | collective-permute-start | bytes 196616 | tf_op jit(solution)/shard_map/ppermute | solution.py:21
  60.7 8.4 %collective-permute-start.7 = (bf16[2,16,8,128]{3,1,2,0:T(8,128)(2,1)S(1)}, bf16[2,16,8,128]{3,1,2,0:T(8,128)(2,1)S(1)}, u32[]{:S(2)}, u32[]{:S(2)}) collective-permute-start(bf16[2,16,8,128]{3,1,2,0:T(8,128)(2,1)S(1)} %get-tuple-element.124), channel_id=1, source_target_pairs={{1,0},{2,1},{3,2},{4,3},{5,4},{6,5},{7,6},{9,8},{10,9},{11,10},{12... | collective-permute-start | bytes 196616 | tf_op jit(solution)/shard_map/ppermute | solution.py:23
  62.7 120.9 %reduce-scatter.2.cloned.1.call-start = ((), (), s32[]{:S(2)}) async-start(), calls=%async_computation.5 | async-start | bytes 147456 | tf_op jit(solution)/shard_map/reduce_scatter | solution.py:120
  71.4 1.1 copy-start.18
  72.4 1.0 copy-start.23
  81.0 1.9 copy-start.6
  82.9 1.3 copy-start.9
  84.7 0.7 copy-start.14
  121.9 62.4 %copy-start.3 = (bf16[3,1024,256]{2,1,0:T(8,128)(2,1)S(1)}, bf16[3,1024,256]{2,1,0:T(8,128)(2,1)}, u32[]{:S(2)}) copy-start(bf16[3,1024,256]{2,1,0:T(8,128)(2,1)} %all-gather.7.cloned.1.call-done) | copy-start | bytes 4718596
  203.3 6.5 %copy-start.15 = (f32[512,128]{1,0:T(8,128)S(1)}, f32[512,128]{1,0:T(8,128)}, u32[]{:S(2)}) copy-start(f32[512,128]{1,0:T(8,128)} %copy-done.14) | copy-start | bytes 786436
  209.8 2.7 copy-start.16
  210.0 5.1 %collective-permute-start.8 = (bf16[8,16,2,128]{3,1,2,0:T(8,128)(2,1)S(1)}, bf16[8,16,2,128]{3,1,2,0:T(8,128)(2,1)S(1)}, u32[]{:S(2)}, u32[]{:S(2)}) collective-permute-start(bf16[8,16,2,128]{3,1,2,0:T(8,128)(2,1)S(1)} %get-tuple-element.129), channel_id=1, source_target_pairs={{0,8},{8,16},{16,24},{1,9},{9,17},{17,25},{2,10},{10,18},{18,26},{... | collective-permute-start | bytes 196616 | tf_op jit(solution)/shard_map/ppermute | solution.py:21
  212.6 5.6 %collective-permute-start.9 = (bf16[8,16,2,128]{3,1,2,0:T(8,128)(2,1)S(1)}, bf16[8,16,2,128]{3,1,2,0:T(8,128)(2,1)S(1)}, u32[]{:S(2)}, u32[]{:S(2)}) collective-permute-start(bf16[8,16,2,128]{3,1,2,0:T(8,128)(2,1)S(1)} %get-tuple-element.130), channel_id=1, source_target_pairs={{8,0},{16,8},{24,16},{9,1},{17,9},{25,17},{10,2},{18,10},{26,18},{... | collective-permute-start | bytes 196616 | tf_op jit(solution)/shard_map/ppermute | solution.py:23
  218.2 15.5 %collective-permute-start.10 = (bf16[2,16,8,128]{3,1,2,0:T(8,128)(2,1)S(1)}, bf16[2,16,8,128]{3,1,2,0:T(8,128)(2,1)S(1)}, u32[]{:S(2)}, u32[]{:S(2)}) collective-permute-start(bf16[2,16,8,128]{3,1,2,0:T(8,128)(2,1)S(1)} %get-tuple-element.121), channel_id=1, source_target_pairs={{0,1},{1,2},{2,3},{3,4},{4,5},{5,6},{6,7},{8,9},{9,10},{10,11},{11... | collective-permute-start | bytes 196616 | tf_op jit(solution)/shard_map/ppermute | solution.py:21
  227.1 6.6 %collective-permute-start.11 = (bf16[2,16,8,128]{3,1,2,0:T(8,128)(2,1)S(1)}, bf16[2,16,8,128]{3,1,2,0:T(8,128)(2,1)S(1)}, u32[]{:S(2)}, u32[]{:S(2)}) collective-permute-start(bf16[2,16,8,128]{3,1,2,0:T(8,128)(2,1)S(1)} %get-tuple-element.122), channel_id=1, source_target_pairs={{1,0},{2,1},{3,2},{4,3},{5,4},{6,5},{7,6},{9,8},{10,9},{11,10},{12... | collective-permute-start | bytes 196616 | tf_op jit(solution)/shard_map/ppermute | solution.py:23
  235.9 1.0 copy-start.19
  237.0 1.0 copy-start.24
  243.8 1.5 copy-start.28
  245.3 1.3 copy-start.4
  245.3 1.3 copy-start.26
  245.8 1.3 copy-start.13
  245.8 1.3 copy-start.17
  245.8 1.3 copy-start.32
  247.1 15.5 %copy-start.10 = (bf16[1,3456,128]{2,1,0:T(8,128)(2,1)S(1)}, bf16[1,3456,128]{2,1,0:T(8,128)(2,1)}, u32[]{:S(2)}) copy-start(bf16[1,3456,128]{2,1,0:T(8,128)(2,1)} %get-tuple-element.7) | copy-start | bytes 2654212
  247.9 6.0 %collective-permute-start.12 = (bf16[8,16,2,128]{3,1,2,0:T(8,128)(2,1)S(1)}, bf16[8,16,2,128]{3,1,2,0:T(8,128)(2,1)S(1)}, u32[]{:S(2)}, u32[]{:S(2)}) collective-permute-start(bf16[8,16,2,128]{3,1,2,0:T(8,128)(2,1)S(1)} %get-tuple-element.127), channel_id=1, source_target_pairs={{0,8},{8,16},{16,24},{1,9},{9,17},{17,25},{2,10},{10,18},{18,26},{... | collective-permute-start | bytes 196616 | tf_op jit(solution)/shard_map/ppermute | solution.py:21
  252.1 5.9 %collective-permute-start.13 = (bf16[8,16,2,128]{3,1,2,0:T(8,128)(2,1)S(1)}, bf16[8,16,2,128]{3,1,2,0:T(8,128)(2,1)S(1)}, u32[]{:S(2)}, u32[]{:S(2)}) collective-permute-start(bf16[8,16,2,128]{3,1,2,0:T(8,128)(2,1)S(1)} %get-tuple-element.128), channel_id=1, source_target_pairs={{8,0},{16,8},{24,16},{9,1},{17,9},{25,17},{10,2},{18,10},{26,18},{... | collective-permute-start | bytes 196616 | tf_op jit(solution)/shard_map/ppermute | solution.py:23
  258.0 7.4 %collective-permute-start.14 = (bf16[2,16,8,128]{3,1,2,0:T(8,128)(2,1)S(1)}, bf16[2,16,8,128]{3,1,2,0:T(8,128)(2,1)S(1)}, u32[]{:S(2)}, u32[]{:S(2)}) collective-permute-start(bf16[2,16,8,128]{3,1,2,0:T(8,128)(2,1)S(1)} %get-tuple-element.119), channel_id=1, source_target_pairs={{0,1},{1,2},{2,3},{3,4},{4,5},{5,6},{6,7},{8,9},{9,10},{10,11},{11... | collective-permute-start | bytes 196616 | tf_op jit(solution)/shard_map/ppermute | solution.py:21
  260.4 5.6 %collective-permute-start.15 = (bf16[2,16,8,128]{3,1,2,0:T(8,128)(2,1)S(1)}, bf16[2,16,8,128]{3,1,2,0:T(8,128)(2,1)S(1)}, u32[]{:S(2)}, u32[]{:S(2)}) collective-permute-start(bf16[2,16,8,128]{3,1,2,0:T(8,128)(2,1)S(1)} %get-tuple-element.120), channel_id=1, source_target_pairs={{1,0},{2,1},{3,2},{4,3},{5,4},{6,5},{7,6},{9,8},{10,9},{11,10},{12... | collective-permute-start | bytes 196616 | tf_op jit(solution)/shard_map/ppermute | solution.py:23
  268.2 1.0 copy-start.20
  269.2 1.0 copy-start.25
  276.0 1.5 copy-start.29
  277.5 1.3 copy-start.5
  277.5 1.3 copy-start.27
  278.1 1.3 copy-start.30
  278.1 2.0 copy-start.1
Sparse Core Ops, SparseCore 0:
  9.0 85.8 all-gather.4
  96.5 23.6 all-gather.6
  157.8 25.7 reduce-scatter.1
where the time goes:
time: 288 us; the launch traced here: 287 us
  blocking collectives  67.8 us (24%)
  local copies, waits for them, and re-layouts  59.7 us (21%)
  waiting for transfers between devices  54.3 us (19%)
  starting transfers between devices  50.3 us (17%)
  between operations  25.2 us (9%)
  matrix products  25 us (9%)
  other arithmetic  4.33 us (2%)
    ppermute x8, starting transfers between devices, padded_2(): lax.ppermute(tail, axis, [(i, (i + 1) % count) for i in range(ends)])  34.8 us
    psum x2, blocking collectives, slab_total(): return lax.psum(term.astype(jnp.bfloat16), 'zslab').astype(jnp.float32)  26.5 us
    reduce_scatter x1, waiting for transfers between devices, local(): lax.psum_scatter(jnp.concatenate([key_term.reshape(lax.axis_size('blk') *...  25.7 us
    unnamed x106, local copies, waits for them, and re-layouts  20.3 us
    ppermute x8, waiting for transfers between devices, padded_2(): lax.ppermute(head, axis, [((i + 1) % count, i) for i in range(ends)])  17.7 us
    ppermute x8, starting transfers between devices, padded_2(): lax.ppermute(head, axis, [((i + 1) % count, i) for i in range(ends)])  15.2 us
    all_gather x1, blocking collectives, local(): lax.all_gather(projected[1], 'blk', axis=0, tiled=True)  14.2 us
    all_gather x1, blocking collectives, local(): lax.all_gather(projected[2], 'blk', axis=0, tiled=True)  14 us
  transfers between devices with their start and end apart: 19, of which 11 were waited for; matrix products, arithmetic and copies ran while one was open for 13% of the time, Pallas kernels for 0%

commit v1 on v0

--- a/solution.py
+++ b/solution.py
@@ -1,6 +1,10 @@
+import functools
+
 import jax
 import jax.numpy as jnp
 from jax import lax
+from jax.experimental import pallas as pl
+from jax.experimental.pallas import tpu as pltpu
 from jax.sharding import PartitionSpec as P
 
 HD = 128
@@ -167,9 +171,432 @@
     return grid_grad
 
 
+HALO = [(dz, dx) for dz in (-1, 0, 1) for dx in (-1, 0, 1) if (dz, dx) != (0, 0)]
+ZS = 4
+NB = 8
+ND = ZS * NB
+ZC, XC, YC, C = 4, 8, 16, 128
+CELLS = ZC * XC * YC
+F32 = jnp.float32
+BF16 = jnp.bfloat16
+CONTRACT_LAST = (((1,), (1,)), ((), ()))
+
+
+def one_hot(target):
+    rows = lax.broadcasted_iota(jnp.int32, (CELLS, 1), 0)
+    cols = lax.broadcasted_iota(jnp.int32, (CELLS, CELLS), 1)
+    return jnp.where(cols == target(rows), 1.0, 0.0).astype(F32).astype(BF16)
+
+
+def bit(value, low, count):
+    return (value >> low) & ((1 << count) - 1)
+
+
+def cell_of_slot(r):
+    zs, py, px_lo, pz, yp, zp_lo = (
+        bit(r, 7, 2), bit(r, 4, 3), bit(r, 3, 1), bit(r, 2, 1), bit(r, 1, 1), bit(r, 0, 1)
+    )
+    return (zp_lo * 2 + pz) * 128 + (2 * zs + px_lo) * 16 + yp * 8 + py
+
+
+def slot_of_cell(r):
+    zp_lo, pz, zs, px_lo, yp, py = (
+        bit(r, 8, 1), bit(r, 7, 1), bit(r, 5, 2), bit(r, 4, 1), bit(r, 3, 1), bit(r, 0, 3)
+    )
+    return (zs * 8 + py) * 16 + px_lo * 8 + pz * 4 + yp * 2 + zp_lo
+
+
+def arrival_of_row(r):
+    q, xp, yp, zs, zp_lo = bit(r, 7, 2), bit(r, 4, 3), bit(r, 3, 1), bit(r, 1, 2), bit(r, 0, 1)
+    return (zs * 8 + xp) * 16 + q * 4 + yp * 2 + zp_lo
+
+
+def row_of_arrival(r):
+    zs, xp, q, yp, zp_lo = bit(r, 7, 2), bit(r, 4, 3), bit(r, 2, 2), bit(r, 1, 1), bit(r, 0, 1)
+    return q * 128 + xp * 16 + yp * 8 + zs * 2 + zp_lo
+
+
+def sigmoid(a):
+    return 1.0 / (1.0 + jnp.exp(-a))
+
+
+def span(step, size):
+    if step == 0:
+        return 2, 2, size
+    return (size, 0, 2) if step == 1 else (2, size + 2, 2)
+
+
+def kernel(
+    dilation, field, mask, conv_hbm, embed_hbm, qkv_hbm, grad_hbm, out,
+    pads, taps, conv_w, embed, weights, grads, conv_outs,
+    send_patch, got_patch, send_part, got_part, tokens,
+    send_gt, got_gt, grad_tok, send_back, got_back,
+    halo_send, halo_recv, load_sem, qkv_send, qkv_recv, fwd_send, fwd_recv,
+    og_send, og_recv, all_send, all_recv, gt_send, gt_recv,
+):
+    zs, b = lax.axis_index("zslab"), lax.axis_index("blk")
+    me = zs * NB + b
+    partner = b + 1 - 2 * lax.rem(b, 2)
+
+    loads = [
+        pltpu.make_async_copy(conv_hbm, conv_w, load_sem.at[0]),
+        pltpu.make_async_copy(embed_hbm, embed, load_sem.at[1]),
+        pltpu.make_async_copy(qkv_hbm, weights.at[b], load_sem.at[2]),
+        pltpu.make_async_copy(grad_hbm, grads.at[b], load_sem.at[3]),
+    ]
+    for load in loads:
+        load.start()
+
+    pads[...] = jnp.zeros_like(pads)
+    barrier = pltpu.get_barrier_semaphore()
+
+    @pl.loop(1, ND)
+    def _(d):
+        peer = lax.rem(me + d, ND)
+        pl.semaphore_signal(
+            barrier, inc=1, device_id=(peer // NB, lax.rem(peer, NB)),
+            device_id_type=pl.DeviceIdType.MESH,
+        )
+
+    pl.semaphore_wait(barrier, ND - 1)
+
+    def remote(src, dst, send, recv, to):
+        return pltpu.make_async_remote_copy(
+            src_ref=src, dst_ref=dst, send_sem=send, recv_sem=recv,
+            device_id=to, device_id_type=pl.DeviceIdType.MESH,
+        )
+
+    def halo_copy(n, d):
+        dz, dx = HALO[d]
+        z0, z1, zl = span(dz, ZC)
+        x0, x1, xl = span(dx, XC)
+        return remote(
+            pads.at[n, pl.ds(z0, zl), pl.ds(x0, xl)], pads.at[n, pl.ds(z1, zl), pl.ds(x1, xl)],
+            halo_send.at[n, d], halo_recv.at[n, d],
+            (lax.rem(zs + dz + ZS, ZS), lax.rem(b + dx + NB, NB)),
+        )
+
+    def inside(dz, dx):
+        return (zs + dz >= 0) & (zs + dz < ZS) & (b + dx >= 0) & (b + dx < NB)
+
+    def send_halo(n, cells):
+        pads[n, 2:6, 2:10] = cells.reshape(ZC, XC, YC, C)
+        for d, (dz, dx) in enumerate(HALO):
+            @pl.when(inside(dz, dx))
+            def _():
+                halo_copy(n, d).start()
+
+    def wait_halo(n):
+        for d, (dz, dx) in enumerate(HALO):
+            @pl.when(inside(-dz, -dx))
+            def _():
+                halo_copy(n, d).wait_recv()
+
+            @pl.when(inside(dz, dx))
+            def _():
+                halo_copy(n, d).wait_send()
+
+    def convolve(n, layer, direction):
+        rx, ry, rz = dilation[layer, 0], dilation[layer, 1], dilation[layer, 2]
+        rows = (ZC + 4) * (XC + 4) * YC
+        flat = pads[n].reshape(rows, C).astype(F32)
+        y = lax.broadcasted_iota(jnp.int32, (rows, C), 0) & (YC - 1)
+
+        def shifted(by):
+            near = pltpu.roll(flat, (-by) % rows, 0)
+            far = pltpu.roll(flat, (-2 * by) % rows, 0)
+            moved = jnp.where(ry == 1, near, far)
+            source = y + by * ry
+            return jnp.where((source >= 0) & (source < YC), moved, 0.0)
+
+        for j, value in ((0, shifted(-direction)), (1, flat), (2, shifted(direction))):
+            taps[:, :, :, j * C:(j + 1) * C] = value.astype(BF16).reshape(
+                ZC + 4, XC + 4, YC, C
+            )
+        total = jnp.zeros((CELLS, C), F32)
+        for i in (-1, 0, 1):
+            for k in (-1, 0, 1):
+                lhs = taps[
+                    pl.ds(2 + direction * k * rz, ZC), pl.ds(2 + direction * i * rx, XC)
+                ].reshape(CELLS, 3 * C)
+                rows_at = [(9 * (i + 1) + 3 * j + k + 1) * C for j in range(3)]
+                parts = [conv_w[layer, at:at + C, :] for at in rows_at]
+                if direction == 1:
+                    total += jnp.dot(
+                        lhs, jnp.concatenate(parts, axis=0), preferred_element_type=F32
+                    )
+                else:
+                    total += lax.dot_general(
+                        lhs, jnp.concatenate(parts, axis=1), CONTRACT_LAST,
+                        preferred_element_type=F32,
+                    )
+        return total
+
+    def all_copy(phase, d, src, dst):
+        peer = lax.rem(me + d, ND)
+        return remote(
+            src, dst, all_send.at[phase, d], all_recv.at[phase, d],
+            (peer // NB, lax.rem(peer, NB)),
+        )
+
+    def scatter(phase, sends, gets):
+        @pl.loop(1, ND)
+        def _(d):
+            all_copy(phase, d, sends.at[lax.rem(me + d, ND)], gets.at[me]).start()
+
+        gets[pl.ds(me, 1)] = sends[pl.ds(me, 1)]
+
+    def scatter_wait(phase, sends, gets):
+        @pl.loop(1, ND)
+        def _(d):
+            copy = all_copy(
+                phase, d, sends.at[lax.rem(me + d, ND)], gets.at[lax.rem(me - d + ND, ND)]
+            )
+            copy.wait_recv()
+            copy.wait_send()
+
+    send_halo(0, field[...])
+
+    def qkv_copy(d):
+        return remote(
+            qkv_hbm, weights.at[b], qkv_send.at[d], qkv_recv.at[d],
+            (zs, partner if d == 0 else lax.rem(b + 2 * d, NB)),
+        )
+
+    def qkv_forward(d):
+        held = weights.at[lax.rem(b - 2 * d + NB, NB)]
+        return remote(held, held, fwd_send.at[d], fwd_recv.at[d], (zs, partner))
+
+    def grad_copy(d):
+        return remote(
+            grad_hbm, grads.at[b], og_send.at[d], og_recv.at[d], (zs, lax.rem(b + d, NB))
+        )
+
+    for d in range(NB // 2):
+        qkv_copy(d).start()
+    for d in range(1, NB):
+        grad_copy(d).start()
+
+    gate = mask[...]
+    loads[0].wait()
+    hidden = field[...].reshape(CELLS, C)
+    for layer in range(LAYERS):
+        if layer:
+            send_halo(layer, hidden)
+        wait_halo(layer)
+        conv_out = convolve(layer, layer, 1)
+        conv_outs[layer] = conv_out
+        hidden = (hidden.astype(F32) + gate * (conv_out * sigmoid(conv_out))).astype(BF16)
+
+    send_patch[...] = (
+        jnp.dot(one_hot(cell_of_slot), hidden, preferred_element_type=F32)
+        .astype(BF16).reshape(ND, 16, C)
+    )
+    scatter(0, send_patch, got_patch)
+    for d in range(1, NB // 2):
+        qkv_copy(d).wait_recv()
+        qkv_forward(d).start()
+    loads[1].wait()
+    gather_rows = one_hot(arrival_of_row)
+    scatter_wait(0, send_patch, got_patch)
+    ordered = jnp.dot(
+        gather_rows, got_patch[...].reshape(CELLS, C), preferred_element_type=F32
+    ).astype(BF16)
+    patches = jnp.concatenate([ordered[q * 128:(q + 1) * 128] for q in range(4)], axis=1)
+    for part in range(ZS):
+        columns = slice(part * 256, (part + 1) * 256)
+        send_part[part * NB:(part + 1) * NB] = (
+            jnp.dot(patches, embed[:, columns], preferred_element_type=F32)
+            .astype(BF16).reshape(NB, 16, 256)
+        )
+    scatter(1, send_part, got_part)
+    scatter_wait(1, send_part, got_part)
+    tokens[pl.ds(me, 1)] = (
+        jnp.sum(got_part[...].astype(F32), axis=0, keepdims=True).astype(BF16)
+    )
+
+    @pl.loop(1, ND)
+    def _(d):
+        all_copy(2, d, tokens.at[me], tokens.at[me]).start()
+
+    for load in loads[2:]:
+        load.wait()
+    qkv_copy(0).wait()
+    for d in range(1, NB // 2):
+        qkv_copy(d).wait_send()
+        qkv_forward(d).wait_send()
+        remote(
+            qkv_hbm, weights.at[lax.rem(partner - 2 * d + NB, NB)],
+            fwd_send.at[d], fwd_recv.at[d], (zs, partner),
+        ).wait_recv()
+    for d in range(1, NB):
+        grad_copy(d).wait()
+
+    @pl.loop(1, ND)
+    def _(d):
+        held = tokens.at[lax.rem(me - d + ND, ND)]
+        copy = all_copy(2, d, held, held)
+        copy.wait_recv()
+        copy.wait_send()
+
+    all_tokens = jnp.concatenate(
+        [tokens[part * NB:(part + 1) * NB].reshape(128, 256) for part in range(ZS)], axis=1
+    )
+    projected = [
+        jnp.dot(all_tokens, weights[:, s].reshape(1024, 256), preferred_element_type=F32)
+        .astype(BF16)
+        for s in range(3)
+    ]
+    grad_out = grads[...].reshape(128, 256)
+    inv_root = HD ** (-0.5)
+    pieces = []
+    for head in range(2):
+        columns = slice(head * HD, (head + 1) * HD)
+        query, key, value = (array[:, columns] for array in projected)
+        grad_h = grad_out[:, columns]
+        scores = lax.dot_general(query, key, CONTRACT_LAST, preferred_element_type=F32) * inv_root
+        expo = jnp.exp(scores - jnp.max(scores, axis=1, keepdims=True))
+        probs = expo / jnp.sum(expo, axis=1, keepdims=True)
+        probs_b = probs.astype(BF16)
+        attended = jnp.dot(probs_b, value, preferred_element_type=F32)
+        row_delta = jnp.sum(grad_h.astype(F32) * attended, axis=1, keepdims=True)
+        score_grad = lax.dot_general(grad_h, value, CONTRACT_LAST, preferred_element_type=F32)
+        dscore = probs * (score_grad - row_delta) * inv_root
+        dscore_t = dscore.T.astype(BF16)
+        probs_t = probs.T.astype(BF16)
+        pieces.append((
+            jnp.dot(dscore.astype(BF16), key, preferred_element_type=F32).astype(BF16),
+            jnp.dot(dscore_t, query, preferred_element_type=F32).astype(BF16),
+            jnp.dot(probs_t, grad_h, preferred_element_type=F32).astype(BF16),
+        ))
+    stacked = [jnp.concatenate([piece[s] for piece in pieces], axis=1) for s in range(3)]
+    for part in range(ZS):
+        term = jnp.zeros((128, 256), F32)
+        for s in range(3):
+            rows = weights[part * 2:part * 2 + 2, s].reshape(256, 256)
+            term += lax.dot_general(stacked[s], rows, CONTRACT_LAST, preferred_element_type=F32)
+        send_gt[part] = term.astype(BF16)
+
+    def slab_copy(phase, d, src, dst):
+        return remote(
+            src, dst, gt_send.at[phase, d], gt_recv.at[phase, d], (lax.rem(zs + d, ZS), b)
+        )
+
+    for d in range(1, ZS):
+        slab_copy(0, d, send_gt.at[lax.rem(zs + d, ZS)], got_gt.at[zs]).start()
+    got_gt[pl.ds(zs, 1)] = send_gt[pl.ds(zs, 1)]
+    for d in range(1, ZS):
+        slab_copy(
+            0, d, send_gt.at[lax.rem(zs + d, ZS)], got_gt.at[lax.rem(zs - d + ZS, ZS)]
+        ).wait()
+    grad_tok[pl.ds(zs, 1)] = (
+        jnp.sum(got_gt[...].astype(F32), axis=0, keepdims=True).astype(BF16)
+    )
+    for d in range(1, ZS):
+        slab_copy(1, d, grad_tok.at[zs], grad_tok.at[zs]).start()
+    scatter_rows = one_hot(row_of_arrival)
+    for d in range(1, ZS):
+        held = grad_tok.at[lax.rem(zs - d + ZS, ZS)]
+        slab_copy(1, d, held, held).wait()
+    all_grad = jnp.concatenate([grad_tok[part] for part in range(ZS)], axis=1)
+    patch_grad = jnp.concatenate(
+        [
+            lax.dot_general(
+                all_grad, embed[q * 128:(q + 1) * 128, :], CONTRACT_LAST,
+                preferred_element_type=F32,
+            ).astype(BF16)
+            for q in range(4)
+        ],
+        axis=0,
+    )
+    send_back[...] = (
+        jnp.dot(scatter_rows, patch_grad, preferred_element_type=F32)
+        .astype(BF16).reshape(ND, 16, C)
+    )
+    scatter(3, send_back, got_back)
+    to_cells = one_hot(slot_of_cell)
+    scatter_wait(3, send_back, got_back)
+    grid_grad = jnp.dot(to_cells, got_back[...].reshape(CELLS, C), preferred_element_type=F32)
+    for layer in reversed(range(LAYERS)):
+        conv_out = conv_outs[layer]
+        sigma = sigmoid(conv_out)
+        slope = gate * sigma * (1.0 + conv_out * (1.0 - sigma)) * grid_grad
+        n = 2 * LAYERS - 1 - layer
+        send_halo(n, slope.astype(BF16))
+        wait_halo(n)
+        grid_grad = (grid_grad + convolve(n, layer, -1)).astype(BF16).astype(F32)
+    out[...] = grid_grad.astype(BF16).reshape(ZC, XC, YC, C)
+
+
+def fused(field, fracture_mask, dilation, conv_weight, embed_weight, qkv_weight, out_grad):
+    cells = field.transpose(2, 0, 1, 3)
+    gate = jnp.broadcast_to(
+        fracture_mask.transpose(2, 0, 1).reshape(CELLS, 1).astype(F32), (CELLS, C)
+    )
+    vmem = pl.BlockSpec(memory_space=pltpu.VMEM)
+    hbm = pl.BlockSpec(memory_space=pl.ANY)
+    dma = pltpu.SemaphoreType.DMA
+    result = pl.pallas_call(
+        kernel,
+        out_shape=jax.ShapeDtypeStruct(cells.shape, BF16),
+        in_specs=[pl.BlockSpec(memory_space=pltpu.SMEM), vmem, vmem, hbm, hbm, hbm, hbm],
+        out_specs=vmem,
+        scratch_shapes=[
+            pltpu.VMEM((2 * LAYERS, ZC + 4, XC + 4, YC, C), BF16),
+            pltpu.VMEM((ZC + 4, XC + 4, YC, 3 * C), BF16),
+            pltpu.VMEM(conv_weight.shape, BF16),
+            pltpu.VMEM((512, 1024), BF16),
+            pltpu.VMEM((NB, 3, 128, 256), BF16),
+            pltpu.VMEM((NB, 16, 256), BF16),
+            pltpu.VMEM((LAYERS, CELLS, C), F32),
+            pltpu.VMEM((ND, 16, C), BF16),
+            pltpu.VMEM((ND, 16, C), BF16),
+            pltpu.VMEM((ND, 16, 256), BF16),
+            pltpu.VMEM((ND, 16, 256), BF16),
+            pltpu.VMEM((ND, 16, 256), BF16),
+            pltpu.VMEM((ZS, 128, 256), BF16),
+            pltpu.VMEM((ZS, 128, 256), BF16),
+            pltpu.VMEM((ZS, 128, 256), BF16),
+            pltpu.VMEM((ND, 16, C), BF16),
+            pltpu.VMEM((ND, 16, C), BF16),
+            dma((2 * LAYERS, 8)),
+            dma((2 * LAYERS, 8)),
+            dma((4,)),
+            dma((NB // 2,)),
+            dma((NB // 2,)),
+            dma((NB // 2,)),
+            dma((NB // 2,)),
+            dma((NB,)),
+            dma((NB,)),
+            dma((4, ND)),
+            dma((4, ND)),
+            dma((2, ZS)),
+            dma((2, ZS)),
+        ],
+        compiler_params=pltpu.CompilerParams(
+            collective_id=0, has_side_effects=True, vmem_limit_bytes=48 * 1024 * 1024
+        ),
+    )(
+        dilation, cells, gate, conv_weight, embed_weight.reshape(512, 1024), qkv_weight, out_grad
+    )
+    return result.transpose(1, 2, 0, 3)
+
+
+def block(*arrays):
+    field, embed_weight, qkv_weight, out_grad = (arrays[0], arrays[4], arrays[5], arrays[6])
+    fits = (
+        (lax.axis_size("zslab"), lax.axis_size("blk")) == (ZS, NB)
+        and field.shape == (XC, YC, ZC, C)
+        and embed_weight.shape == (2, 256, 1024)
+        and qkv_weight.shape == (3, 128, 256)
+        and out_grad.shape == (16, 256)
+    )
+    return fused(*arrays) if fits else local(*arrays)
+
+
 def solution(mesh):
     return jax.shard_map(
-        local,
+        block,
         mesh=mesh,
         in_specs=(
             P("blk", None, "zslab", None),

time: 288 us -> 97.7 us (0.34)
  Pallas kernels: 0 us -> 89 us
  blocking collectives: 67.8 us -> 0 us
  waiting for transfers between devices: 54.3 us -> 0 us
  local copies, waits for them, and re-layouts: 59.7 us -> 6.89 us
  starting transfers between devices: 50.3 us -> 0 us
  between operations: 25.2 us -> 0.03 us
  matrix products: 25 us -> 0 us
  other arithmetic: 4.33 us -> 0.72 us
    pallas_call x0 -> x1, Pallas kernels: none -> 89 us  [fused(): pl.pallas_call(kernel, out_shape=jax.ShapeDtypeStruct(cells.shape, BF16),...]
    ppermute x16 -> x0, starting transfers between devices: 50 us -> none  [the longest x8 34.8 us: padded_2(): lax.ppermute(tail, axis, [(i, (i + 1) % count) for i in range(ends)])]
    all_gather x2 -> x0, blocking collectives: 28.2 us -> none  [the longest x1 14.2 us: local(): lax.all_gather(projected[1], 'blk', axis=0, tiled=True)]
    psum x2 -> x0, blocking collectives: 26.5 us -> none  [slab_total(): return lax.psum(term.astype(jnp.bfloat16), 'zslab').astype(jnp.float32)]
    reduce_scatter x1 -> x0, waiting for transfers between devices: 25.7 us -> none  [local(): lax.psum_scatter(jnp.concatenate([key_term.reshape(lax.axis_size('blk') *...]
    dot_general x22 -> x0, matrix products: 25 us -> none  [the longest x12 9.11 us: apply_offsets(): jnp.dot(stacked, group_rows, preferred_element_type=jnp.float32)]
    ppermute x16 -> x0, waiting for transfers between devices: 18.2 us -> none  [the longest x8 17.7 us: padded_2(): lax.ppermute(head, axis, [((i + 1) % count, i) for i in range(ends)])]
    reshape x19 -> x0, local copies, waits for them, and re-layouts: 16.5 us -> none  [the longest x12 14 us: apply_offsets(): jnp.concatenate(pieces, axis=3)]
  transfers between devices with their start and end apart: 19 -> 0, of which waited for: 11 -> 0; matrix products, arithmetic and copies ran while one was open for 13% -> 0% of each run, Pallas kernels for 0% -> 0%
where the time goes in v1:
time: 97.7 us; the launch traced here: 96.6 us
  Pallas kernels  89 us (91%)
  local copies, waits for them, and re-layouts  6.89 us (7%)
    pallas_call x1, Pallas kernels, fused(): pl.pallas_call(kernel, out_shape=jax.ShapeDtypeStruct(cells.shape, BF16),...  89 us
    unnamed x11, local copies, waits for them, and re-layouts  5.93 us

profile of v1, /device:TPU:1, one launch (start us, length us, event | category | flops | bytes accessed | tf_op | source)
XLA Modules:
  0.0 96.6 jit_solution(13205924431993116096)
XLA Ops:
  0.0 0.7 convert_bitcast_fusion
  0.7 0.1 convert_element_type.16
  0.8 0.9 copy.14
  1.7 0.1 broadcast_in_dim.2.mask
  1.9 0.0 copy-start
  1.9 1.5 %copy-done = bf16[2,3456,128]{2,1,0:T(8,128)(2,1)S(1)} copy-done((bf16[2,3456,128]{2,1,0:T(8,128)(2,1)S(1)}, bf16[2,3456,128]{2,1,0:T(8,128)(2,1)}, u32[]{:S(2)}) %copy-start) | copy-done | bytes 1769496
  3.4 0.0 copy-start.1
  3.4 1.2 %copy-done.1 = bf16[2,256,1024]{2,1,0:T(8,128)(2,1)S(1)} copy-done((bf16[2,256,1024]{2,1,0:T(8,128)(2,1)S(1)}, bf16[2,256,1024]{2,1,0:T(8,128)(2,1)}, u32[]{:S(2)}) %copy-start.1) | copy-done | bytes 1048600
  4.6 0.0 copy-start.2
  4.6 0.9 copy-done.2
  5.5 0.0 copy-start.3
  5.5 0.7 copy-done.3
  6.2 0.0 copy-start.4
  6.2 0.7 copy-done.4
  6.9 89.0 %shard_map.73 = bf16[4,8,16,128]{3,2,1,0:T(8,128)(2,1)S(1)} custom-call(s32[2,3]{1,0:T(2,128)S(1)} %copy-done.4, bf16[4,8,16,128]{3,2,1,0:T(8,128)(2,1)S(1)} %bitcast.8, f32[512,128]{1,0:T(8,128)S(1)} %broadcast_in_dim.2.mask, bf16[2,3456,128]{2,1,0:T(8,128)(2,1)S(1)} %copy-done, bf16[512,1024]{1,0:T(8,128)(2,1)S(1)} %bitcast.7, ...), custom_call_target="tpu_custom_call" | custom-call | tf_op jit(solution)/shard_map/pallas_call | solution.py:539
  95.9 0.8 copy.12
  (1 shorter events, 0.0 us)
Async XLA Ops:
  1.9 1.5 %copy-start = (bf16[2,3456,128]{2,1,0:T(8,128)(2,1)S(1)}, bf16[2,3456,128]{2,1,0:T(8,128)(2,1)}, u32[]{:S(2)}) copy-start(bf16[2,3456,128]{2,1,0:T(8,128)(2,1)} %conv_hbm.1) | copy-start | bytes 5308420
  3.4 1.2 %copy-start.1 = (bf16[2,256,1024]{2,1,0:T(8,128)(2,1)S(1)}, bf16[2,256,1024]{2,1,0:T(8,128)(2,1)}, u32[]{:S(2)}) copy-start(bf16[2,256,1024]{2,1,0:T(8,128)(2,1)} %param.11) | copy-start | bytes 3145732
  4.6 0.9 copy-start.2
  5.5 0.7 copy-start.3
  6.2 0.7 copy-start.4

commit v2 on v1

--- a/solution.py
+++ b/solution.py
@@ -228,12 +228,13 @@
 
 def kernel(
     dilation, field, mask, conv_hbm, embed_hbm, qkv_hbm, grad_hbm, out,
-    pads, taps, conv_w, embed, weights, grads, conv_outs,
+    pad_0, pad_1, pad_2, pad_3, gate_ref, orders, conv_w, embed, weights, grads, conv_outs,
     send_patch, got_patch, send_part, got_part, tokens,
     send_gt, got_gt, grad_tok, send_back, got_back,
     halo_send, halo_recv, load_sem, qkv_send, qkv_recv, fwd_send, fwd_recv,
     og_send, og_recv, all_send, all_recv, gt_send, gt_recv,
 ):
+    pads = (pad_0, pad_1, pad_2, pad_3)
     zs, b = lax.axis_index("zslab"), lax.axis_index("blk")
     me = zs * NB + b
     partner = b + 1 - 2 * lax.rem(b, 2)
@@ -244,10 +245,12 @@
         pltpu.make_async_copy(qkv_hbm, weights.at[b], load_sem.at[2]),
         pltpu.make_async_copy(grad_hbm, grads.at[b], load_sem.at[3]),
     ]
-    for load in loads:
-        load.start()
-
-    pads[...] = jnp.zeros_like(pads)
+    for pad in pads:
+        pad[...] = jnp.zeros_like(pad)
+    loads += [
+        pltpu.make_async_copy(field, pad_0.at[pl.ds(2, ZC), pl.ds(2, XC)], load_sem.at[4]),
+        pltpu.make_async_copy(mask, gate_ref, load_sem.at[5]),
+    ]
     barrier = pltpu.get_barrier_semaphore()
 
     @pl.loop(1, ND)
@@ -258,6 +261,11 @@
             device_id_type=pl.DeviceIdType.MESH,
         )
 
+    for load in loads[::-1]:
+        load.start()
+    for at, target in enumerate((cell_of_slot, arrival_of_row, row_of_arrival, slot_of_cell)):
+        orders[at] = one_hot(target)
+    loads[4].wait()
     pl.semaphore_wait(barrier, ND - 1)
 
     def remote(src, dst, send, recv, to):
@@ -271,7 +279,7 @@
         z0, z1, zl = span(dz, ZC)
         x0, x1, xl = span(dx, XC)
         return remote(
-            pads.at[n, pl.ds(z0, zl), pl.ds(x0, xl)], pads.at[n, pl.ds(z1, zl), pl.ds(x1, xl)],
+            pads[n].at[pl.ds(z0, zl), pl.ds(x0, xl)], pads[n].at[pl.ds(z1, zl), pl.ds(x1, xl)],
             halo_send.at[n, d], halo_recv.at[n, d],
             (lax.rem(zs + dz + ZS, ZS), lax.rem(b + dx + NB, NB)),
         )
@@ -279,8 +287,7 @@
     def inside(dz, dx):
         return (zs + dz >= 0) & (zs + dz < ZS) & (b + dx >= 0) & (b + dx < NB)
 
-    def send_halo(n, cells):
-        pads[n, 2:6, 2:10] = cells.reshape(ZC, XC, YC, C)
+    def send_halo(n):
         for d, (dz, dx) in enumerate(HALO):
             @pl.when(inside(dz, dx))
             def _():
@@ -292,52 +299,61 @@
             def _():
                 halo_copy(n, d).wait_recv()
 
-            @pl.when(inside(dz, dx))
-            def _():
-                halo_copy(n, d).wait_send()
-
     def convolve(n, layer, direction):
         rx, ry, rz = dilation[layer, 0], dilation[layer, 1], dilation[layer, 2]
-        rows = (ZC + 4) * (XC + 4) * YC
-        flat = pads[n].reshape(rows, C).astype(F32)
-        y = lax.broadcasted_iota(jnp.int32, (rows, C), 0) & (YC - 1)
-
-        def shifted(by):
-            near = pltpu.roll(flat, (-by) % rows, 0)
-            far = pltpu.roll(flat, (-2 * by) % rows, 0)
-            moved = jnp.where(ry == 1, near, far)
+        places = [(i, k) for i in (-1, 0, 1) for k in (-1, 0, 1)]
+        windows = jnp.concatenate(
+            [
+                pads[n][
+                    pl.ds(2 + direction * k * rz, ZC), pl.ds(2 + direction * i * rx, XC)
+                ].reshape(CELLS, C)
+                for i, k in places
+            ],
+            axis=1,
+        )
+
+        def tap(i, j, k):
+            at = (9 * (i + 1) + 3 * j + k + 1) * C
+            return conv_w[layer, at:at + C, :]
+
+        if direction == 1:
+            matrix = jnp.concatenate(
+                [jnp.concatenate([tap(i, j, k) for j in range(3)], axis=1) for i, k in places],
+                axis=0,
+            )
+            summed = jnp.dot(windows, matrix, preferred_element_type=F32)
+        else:
+            matrix = jnp.concatenate(
+                [jnp.concatenate([tap(i, j, k) for i, k in places], axis=1) for j in range(3)],
+                axis=0,
+            )
+            summed = lax.dot_general(
+                windows, matrix, CONTRACT_LAST, preferred_element_type=F32
+            )
+        y = lax.broadcasted_iota(jnp.int32, (CELLS, C), 0) & (YC - 1)
+
+        def shifted(value, by):
+            near = pltpu.roll(value, (-by) % CELLS, 0)
+            far = pltpu.roll(value, (-2 * by) % CELLS, 0)
             source = y + by * ry
-            return jnp.where((source >= 0) & (source < YC), moved, 0.0)
-
-        for j, value in ((0, shifted(-direction)), (1, flat), (2, shifted(direction))):
-            taps[:, :, :, j * C:(j + 1) * C] = value.astype(BF16).reshape(
-                ZC + 4, XC + 4, YC, C
-            )
-        total = jnp.zeros((CELLS, C), F32)
-        for i in (-1, 0, 1):
-            for k in (-1, 0, 1):
-                lhs = taps[
-                    pl.ds(2 + direction * k * rz, ZC), pl.ds(2 + direction * i * rx, XC)
-                ].reshape(CELLS, 3 * C)
-                rows_at = [(9 * (i + 1) + 3 * j + k + 1) * C for j in range(3)]
-                parts = [conv_w[layer, at:at + C, :] for at in rows_at]
-                if direction == 1:
-                    total += jnp.dot(
-                        lhs, jnp.concatenate(parts, axis=0), preferred_element_type=F32
-                    )
-                else:
-                    total += lax.dot_general(
-                        lhs, jnp.concatenate(parts, axis=1), CONTRACT_LAST,
-                        preferred_element_type=F32,
-                    )
-        return total
+            return jnp.where((source >= 0) & (source < YC), jnp.where(ry == 1, near, far), 0.0)
+
+        return (
+            summed[:, C:2 * C]
+            + shifted(summed[:, :C], -direction)
+            + shifted(summed[:, 2 * C:], direction)
+        )
 
     def all_copy(phase, d, src, dst):
         peer = lax.rem(me + d, ND)
         return remote(
-            src, dst, all_send.at[phase, d], all_recv.at[phase, d],
-            (peer // NB, lax.rem(peer, NB)),
-        )
+            src, dst, all_send.at[phase], all_recv.at[phase],
+            (lax.div(peer, NB), lax.rem(peer, NB)),
+        )
+
+    def all_bytes(phase, ref):
+        part = ref.at[pl.ds(0, ND - 1)]
+        return all_copy(phase, 1, part, part)
 
     def scatter(phase, sends, gets):
         @pl.loop(1, ND)
@@ -346,16 +362,7 @@
 
         gets[pl.ds(me, 1)] = sends[pl.ds(me, 1)]
 
-    def scatter_wait(phase, sends, gets):
-        @pl.loop(1, ND)
-        def _(d):
-            copy = all_copy(
-                phase, d, sends.at[lax.rem(me + d, ND)], gets.at[lax.rem(me - d + ND, ND)]
-            )
-            copy.wait_recv()
-            copy.wait_send()
-
-    send_halo(0, field[...])
+    send_halo(0)
 
     def qkv_copy(d):
         return remote(
@@ -377,19 +384,21 @@
     for d in range(1, NB):
         grad_copy(d).start()
 
-    gate = mask[...]
+    loads[5].wait()
+    gate = gate_ref[...]
     loads[0].wait()
-    hidden = field[...].reshape(CELLS, C)
+    hidden = pad_0[2:6, 2:10].reshape(CELLS, C)
     for layer in range(LAYERS):
         if layer:
-            send_halo(layer, hidden)
+            pads[layer][2:6, 2:10] = hidden.reshape(ZC, XC, YC, C)
+            send_halo(layer)
         wait_halo(layer)
         conv_out = convolve(layer, layer, 1)
         conv_outs[layer] = conv_out
         hidden = (hidden.astype(F32) + gate * (conv_out * sigmoid(conv_out))).astype(BF16)
 
     send_patch[...] = (
-        jnp.dot(one_hot(cell_of_slot), hidden, preferred_element_type=F32)
+        jnp.dot(orders[0], hidden, preferred_element_type=F32)
         .astype(BF16).reshape(ND, 16, C)
     )
     scatter(0, send_patch, got_patch)
@@ -397,10 +406,9 @@
         qkv_copy(d).wait_recv()
         qkv_forward(d).start()
     loads[1].wait()
-    gather_rows = one_hot(arrival_of_row)
-    scatter_wait(0, send_patch, got_patch)
+    all_bytes(0, got_patch).wait_recv()
     ordered = jnp.dot(
-        gather_rows, got_patch[...].reshape(CELLS, C), preferred_element_type=F32
+        orders[1], got_patch[...].reshape(CELLS, C), preferred_element_type=F32
     ).astype(BF16)
     patches = jnp.concatenate([ordered[q * 128:(q + 1) * 128] for q in range(4)], axis=1)
     for part in range(ZS):
@@ -410,7 +418,7 @@
             .astype(BF16).reshape(NB, 16, 256)
         )
     scatter(1, send_part, got_part)
-    scatter_wait(1, send_part, got_part)
+    all_bytes(1, got_part).wait_recv()
     tokens[pl.ds(me, 1)] = (
         jnp.sum(got_part[...].astype(F32), axis=0, keepdims=True).astype(BF16)
     )
@@ -419,25 +427,17 @@
     def _(d):
         all_copy(2, d, tokens.at[me], tokens.at[me]).start()
 
-    for load in loads[2:]:
+    for load in loads[2:4]:
         load.wait()
-    qkv_copy(0).wait()
+    qkv_copy(0).wait_recv()
     for d in range(1, NB // 2):
-        qkv_copy(d).wait_send()
-        qkv_forward(d).wait_send()
         remote(
             qkv_hbm, weights.at[lax.rem(partner - 2 * d + NB, NB)],
             fwd_send.at[d], fwd_recv.at[d], (zs, partner),
         ).wait_recv()
     for d in range(1, NB):
-        grad_copy(d).wait()
-
-    @pl.loop(1, ND)
-    def _(d):
-        held = tokens.at[lax.rem(me - d + ND, ND)]
-        copy = all_copy(2, d, held, held)
-        copy.wait_recv()
-        copy.wait_send()
+        grad_copy(d).wait_recv()
+    all_bytes(2, tokens).wait_recv()
 
     all_tokens = jnp.concatenate(
         [tokens[part * NB:(part + 1) * NB].reshape(128, 256) for part in range(ZS)], axis=1
@@ -488,16 +488,15 @@
     for d in range(1, ZS):
         slab_copy(
             0, d, send_gt.at[lax.rem(zs + d, ZS)], got_gt.at[lax.rem(zs - d + ZS, ZS)]
-        ).wait()
+        ).wait_recv()
     grad_tok[pl.ds(zs, 1)] = (
         jnp.sum(got_gt[...].astype(F32), axis=0, keepdims=True).astype(BF16)
     )
     for d in range(1, ZS):
         slab_copy(1, d, grad_tok.at[zs], grad_tok.at[zs]).start()
-    scatter_rows = one_hot(row_of_arrival)
     for d in range(1, ZS):
         held = grad_tok.at[lax.rem(zs - d + ZS, ZS)]
-        slab_copy(1, d, held, held).wait()
+        slab_copy(1, d, held, held).wait_recv()
     all_grad = jnp.concatenate([grad_tok[part] for part in range(ZS)], axis=1)
     patch_grad = jnp.concatenate(
         [
@@ -510,22 +509,39 @@
         axis=0,
     )
     send_back[...] = (
-        jnp.dot(scatter_rows, patch_grad, preferred_element_type=F32)
+        jnp.dot(orders[2], patch_grad, preferred_element_type=F32)
         .astype(BF16).reshape(ND, 16, C)
     )
     scatter(3, send_back, got_back)
-    to_cells = one_hot(slot_of_cell)
-    scatter_wait(3, send_back, got_back)
-    grid_grad = jnp.dot(to_cells, got_back[...].reshape(CELLS, C), preferred_element_type=F32)
+    all_bytes(3, got_back).wait_recv()
+    grid_grad = jnp.dot(orders[3], got_back[...].reshape(CELLS, C), preferred_element_type=F32)
     for layer in reversed(range(LAYERS)):
         conv_out = conv_outs[layer]
         sigma = sigmoid(conv_out)
         slope = gate * sigma * (1.0 + conv_out * (1.0 - sigma)) * grid_grad
         n = 2 * LAYERS - 1 - layer
-        send_halo(n, slope.astype(BF16))
+        pads[n][2:6, 2:10] = slope.astype(BF16).reshape(ZC, XC, YC, C)
+        send_halo(n)
         wait_halo(n)
         grid_grad = (grid_grad + convolve(n, layer, -1)).astype(BF16).astype(F32)
     out[...] = grid_grad.astype(BF16).reshape(ZC, XC, YC, C)
+
+    for n in range(2 * LAYERS):
+        for d, (dz, dx) in enumerate(HALO):
+            @pl.when(inside(dz, dx))
+            def _():
+                halo_copy(n, d).wait_send()
+    for d in range(NB // 2):
+        qkv_copy(d).wait_send()
+        if d:
+            qkv_forward(d).wait_send()
+    for d in range(1, NB):
+        grad_copy(d).wait_send()
+    for phase, ref in enumerate((send_patch, send_part, tokens, send_back)):
+        all_bytes(phase, ref).wait_send()
+    for phase in range(2):
+        for d in range(1, ZS):
+            slab_copy(phase, d, send_gt.at[0], got_gt.at[0]).wait_send()
 
 
 def fused(field, fracture_mask, dilation, conv_weight, embed_weight, qkv_weight, out_grad):
@@ -534,16 +550,17 @@
         fracture_mask.transpose(2, 0, 1).reshape(CELLS, 1).astype(F32), (CELLS, C)
     )
     vmem = pl.BlockSpec(memory_space=pltpu.VMEM)
-    hbm = pl.BlockSpec(memory_space=pl.ANY)
+    hbm = pl.BlockSpec(memory_space=pltpu.HBM)
     dma = pltpu.SemaphoreType.DMA
     result = pl.pallas_call(
         kernel,
         out_shape=jax.ShapeDtypeStruct(cells.shape, BF16),
-        in_specs=[pl.BlockSpec(memory_space=pltpu.SMEM), vmem, vmem, hbm, hbm, hbm, hbm],
+        in_specs=[pl.BlockSpec(memory_space=pltpu.SMEM)] + [hbm] * 6,
         out_specs=vmem,
         scratch_shapes=[
-            pltpu.VMEM((2 * LAYERS, ZC + 4, XC + 4, YC, C), BF16),
-            pltpu.VMEM((ZC + 4, XC + 4, YC, 3 * C), BF16),
+            *[pltpu.VMEM((ZC + 4, XC + 4, YC, C), BF16)] * (2 * LAYERS),
+            pltpu.VMEM((CELLS, C), F32),
+            pltpu.VMEM((4, CELLS, CELLS), BF16),
             pltpu.VMEM(conv_weight.shape, BF16),
             pltpu.VMEM((512, 1024), BF16),
             pltpu.VMEM((NB, 3, 128, 256), BF16),
@@ -561,15 +578,15 @@
             pltpu.VMEM((ND, 16, C), BF16),
             dma((2 * LAYERS, 8)),
             dma((2 * LAYERS, 8)),
-            dma((4,)),
+            dma((6,)),
             dma((NB // 2,)),
             dma((NB // 2,)),
             dma((NB // 2,)),
             dma((NB // 2,)),
             dma((NB,)),
             dma((NB,)),
-            dma((4, ND)),
-            dma((4, ND)),
+            dma((4,)),
+            dma((4,)),
             dma((2, ZS)),
             dma((2, ZS)),
         ],

time: 97.7 us -> 91.5 us (0.937)
  Pallas kernels: 89 us -> 82.6 us
    pallas_call x1, Pallas kernels: 89 us -> 82.6 us  [fused(): pl.pallas_call(kernel, out_shape=jax.ShapeDtypeStruct(cells.shape, BF16),...]
where the time goes in v2:
time: 91.5 us; the launch traced here: 90.2 us
  Pallas kernels  82.6 us (90%)
  local copies, waits for them, and re-layouts  6.89 us (8%)
    pallas_call x1, Pallas kernels, fused(): pl.pallas_call(kernel, out_shape=jax.ShapeDtypeStruct(cells.shape, BF16),...  82.6 us
    unnamed x11, local copies, waits for them, and re-layouts  5.93 us

profile of v2, /device:TPU:1, one launch (start us, length us, event | category | flops | bytes accessed | tf_op | source)
XLA Modules:
  0.0 90.2 jit_solution(3885964641601139103)
XLA Ops:
  0.0 0.7 convert_bitcast_fusion
  0.7 0.1 convert_element_type.16
  0.8 0.9 %copy.14 = bf16[8,16,4,128]{3,1,0,2:T(8,128)(2,1)S(1)} copy(bf16[8,16,4,128]{3,2,1,0:T(4,128)(2,1)} %param.7) | data formatting | bytes 262144 | tf_op args[0]
  1.7 0.1 broadcast_in_dim.2.mask
  1.9 0.0 copy-start
  1.9 1.5 %copy-done = bf16[2,3456,128]{2,1,0:T(8,128)(2,1)S(1)} copy-done((bf16[2,3456,128]{2,1,0:T(8,128)(2,1)S(1)}, bf16[2,3456,128]{2,1,0:T(8,128)(2,1)}, u32[]{:S(2)}) %copy-start) | copy-done | bytes 1769496
  3.4 0.0 copy-start.1
  3.4 1.2 %copy-done.1 = bf16[2,256,1024]{2,1,0:T(8,128)(2,1)S(1)} copy-done((bf16[2,256,1024]{2,1,0:T(8,128)(2,1)S(1)}, bf16[2,256,1024]{2,1,0:T(8,128)(2,1)}, u32[]{:S(2)}) %copy-start.1) | copy-done | bytes 1048600
  4.6 0.0 copy-start.2
  4.6 0.9 %copy-done.2 = bf16[3,128,256]{2,1,0:T(8,128)(2,1)S(1)} copy-done((bf16[3,128,256]{2,1,0:T(8,128)(2,1)S(1)}, bf16[3,128,256]{2,1,0:T(8,128)(2,1)}, u32[]{:S(2)}) %copy-start.2) | copy-done | bytes 196632
  5.5 0.0 copy-start.3
  5.5 0.7 copy-done.3
  6.2 0.0 copy-start.4
  6.2 0.7 copy-done.4
  6.9 82.6 %shard_map.73 = bf16[4,8,16,128]{3,2,1,0:T(8,128)(2,1)S(1)} custom-call(s32[2,3]{1,0:T(2,128)S(1)} %copy-done.4, bf16[4,8,16,128]{3,2,1,0:T(8,128)(2,1)S(1)} %bitcast.8, f32[512,128]{1,0:T(8,128)S(1)} %broadcast_in_dim.2.mask, bf16[2,3456,128]{2,1,0:T(8,128)(2,1)S(1)} %copy-done, bf16[512,1024]{1,0:T(8,128)(2,1)S(1)} %bitcast.7, ...), custom_call_target="tpu_custom_call" | custom-call | tf_op jit(solution)/shard_map/pallas_call | solution.py:555
  89.5 0.8 copy.12
  (1 shorter events, 0.0 us)
Async XLA Ops:
  1.9 1.5 %copy-start = (bf16[2,3456,128]{2,1,0:T(8,128)(2,1)S(1)}, bf16[2,3456,128]{2,1,0:T(8,128)(2,1)}, u32[]{:S(2)}) copy-start(bf16[2,3456,128]{2,1,0:T(8,128)(2,1)} %conv_hbm.1) | copy-start | bytes 5308420
  3.4 1.2 %copy-start.1 = (bf16[2,256,1024]{2,1,0:T(8,128)(2,1)S(1)}, bf16[2,256,1024]{2,1,0:T(8,128)(2,1)}, u32[]{:S(2)}) copy-start(bf16[2,256,1024]{2,1,0:T(8,128)(2,1)} %param.11) | copy-start | bytes 3145732
  4.6 0.9 %copy-start.2 = (bf16[3,128,256]{2,1,0:T(8,128)(2,1)S(1)}, bf16[3,128,256]{2,1,0:T(8,128)(2,1)}, u32[]{:S(2)}) copy-start(bf16[3,128,256]{2,1,0:T(8,128)(2,1)} %qkv_hbm.1) | copy-start | bytes 589828
  5.5 0.7 copy-start.3
  6.2 0.7 copy-start.4

commit v3 on v2

--- a/solution.py
+++ b/solution.py
@@ -233,6 +233,7 @@
     send_gt, got_gt, grad_tok, send_back, got_back,
     halo_send, halo_recv, load_sem, qkv_send, qkv_recv, fwd_send, fwd_recv,
     og_send, og_recv, all_send, all_recv, gt_send, gt_recv,
+    send_row, got_row, row_send, row_recv,
 ):
     pads = (pad_0, pad_1, pad_2, pad_3)
     zs, b = lax.axis_index("zslab"), lax.axis_index("blk")
@@ -417,15 +418,45 @@
             jnp.dot(patches, embed[:, columns], preferred_element_type=F32)
             .astype(BF16).reshape(NB, 16, 256)
         )
-    scatter(1, send_part, got_part)
-    all_bytes(1, got_part).wait_recv()
+    def slab_copy(phase, d, src, dst):
+        return remote(
+            src, dst, gt_send.at[phase, d], gt_recv.at[phase, d], (lax.rem(zs + d, ZS), b)
+        )
+
+    def row_copy(phase, d, src, dst):
+        return remote(
+            src, dst, row_send.at[phase, d], row_recv.at[phase, d], (zs, lax.rem(b + d, NB))
+        )
+
+    for d in range(1, ZS):
+        slab_copy(
+            2, d, send_part.at[pl.ds(lax.rem(zs + d, ZS) * NB, NB)],
+            got_part.at[pl.ds(zs * NB, NB)],
+        ).start()
+    got_part[pl.ds(zs * NB, NB)] = send_part[pl.ds(zs * NB, NB)]
+    for d in range(1, ZS):
+        held = got_part.at[pl.ds(lax.rem(zs - d + ZS, ZS) * NB, NB)]
+        slab_copy(2, d, held, held).wait_recv()
+    send_row[...] = sum(
+        got_part[part * NB:(part + 1) * NB].astype(F32) for part in range(ZS)
+    ).astype(BF16)
+    for d in range(1, NB):
+        row_copy(0, d, send_row.at[lax.rem(b + d, NB)], got_row.at[b]).start()
+    got_row[pl.ds(b, 1)] = send_row[pl.ds(b, 1)]
+    for d in range(1, NB):
+        held = got_row.at[lax.rem(b - d + NB, NB)]
+        row_copy(0, d, held, held).wait_recv()
     tokens[pl.ds(me, 1)] = (
-        jnp.sum(got_part[...].astype(F32), axis=0, keepdims=True).astype(BF16)
-    )
-
-    @pl.loop(1, ND)
-    def _(d):
-        all_copy(2, d, tokens.at[me], tokens.at[me]).start()
+        jnp.sum(got_row[...].astype(F32), axis=0, keepdims=True).astype(BF16)
+    )
+    for d in range(1, NB):
+        row_copy(1, d, tokens.at[me], tokens.at[me]).start()
+    for d in range(1, NB):
+        held = tokens.at[zs * NB + lax.rem(b - d + NB, NB)]
+        row_copy(1, d, held, held).wait_recv()
+    slab = tokens.at[pl.ds(zs * NB, NB)]
+    for d in range(1, ZS):
+        slab_copy(3, d, slab, slab).start()
 
     for load in loads[2:4]:
         load.wait()
@@ -437,7 +468,9 @@
         ).wait_recv()
     for d in range(1, NB):
         grad_copy(d).wait_recv()
-    all_bytes(2, tokens).wait_recv()
+    for d in range(1, ZS):
+        held = tokens.at[pl.ds(lax.rem(zs - d + ZS, ZS) * NB, NB)]
+        slab_copy(3, d, held, held).wait_recv()
 
     all_tokens = jnp.concatenate(
         [tokens[part * NB:(part + 1) * NB].reshape(128, 256) for part in range(ZS)], axis=1
@@ -477,11 +510,6 @@
             term += lax.dot_general(stacked[s], rows, CONTRACT_LAST, preferred_element_type=F32)
         send_gt[part] = term.astype(BF16)
 
-    def slab_copy(phase, d, src, dst):
-        return remote(
-            src, dst, gt_send.at[phase, d], gt_recv.at[phase, d], (lax.rem(zs + d, ZS), b)
-        )
-
     for d in range(1, ZS):
         slab_copy(0, d, send_gt.at[lax.rem(zs + d, ZS)], got_gt.at[zs]).start()
     got_gt[pl.ds(zs, 1)] = send_gt[pl.ds(zs, 1)]
@@ -537,8 +565,14 @@
             qkv_forward(d).wait_send()
     for d in range(1, NB):
         grad_copy(d).wait_send()
-    for phase, ref in enumerate((send_patch, send_part, tokens, send_back)):
+    for phase, ref in ((0, send_patch), (3, send_back)):
         all_bytes(phase, ref).wait_send()
+    for phase in range(2):
+        for d in range(1, NB):
+            row_copy(phase, d, send_row.at[0], got_row.at[0]).wait_send()
+    for d in range(1, ZS):
+        slab_copy(2, d, slab, slab).wait_send()
+        slab_copy(3, d, slab, slab).wait_send()
     for phase in range(2):
         for d in range(1, ZS):
             slab_copy(phase, d, send_gt.at[0], got_gt.at[0]).wait_send()
@@ -587,11 +621,15 @@
             dma((NB,)),
             dma((4,)),
             dma((4,)),
-            dma((2, ZS)),
-            dma((2, ZS)),
+            dma((4, ZS)),
+            dma((4, ZS)),
+            pltpu.VMEM((NB, 16, 256), BF16),
+            pltpu.VMEM((NB, 16, 256), BF16),
+            dma((2, NB)),
+            dma((2, NB)),
         ],
         compiler_params=pltpu.CompilerParams(
-            collective_id=0, has_side_effects=True, vmem_limit_bytes=48 * 1024 * 1024
+            collective_id=0, has_side_effects=True
         ),
     )(
         dilation, cells, gate, conv_weight, embed_weight.reshape(512, 1024), qkv_weight, out_grad

time: 91.5 us -> 90.6 us (level)
  local copies, waits for them, and re-layouts: 6.89 us -> 4.15 us
  Pallas kernels: 82.6 us -> 84.6 us
    unnamed x11 -> x1, local copies, waits for them, and re-layouts: 5.93 us -> 1.58 us
    pallas_call x1, Pallas kernels: 82.6 us -> 84.6 us  [fused(): pl.pallas_call(kernel, out_shape=jax.ShapeDtypeStruct(cells.shape, BF16),...]
where the time goes in v3:
time: 90.6 us; the launch traced here: 89.5 us
  Pallas kernels  84.6 us (93%)
  local copies, waits for them, and re-layouts  4.15 us (5%)
    pallas_call x1, Pallas kernels, fused(): pl.pallas_call(kernel, out_shape=jax.ShapeDtypeStruct(cells.shape, BF16),...  84.6 us

profile of v3, /device:TPU:1, one launch (start us, length us, event | category | flops | bytes accessed | tf_op | source)
XLA Modules:
  0.0 89.5 jit_solution(6476865106872863071)
XLA Ops:
  0.0 0.7 convert_bitcast_fusion
  0.7 0.1 convert_element_type.16
  0.8 1.6 %copy.14 = bf16[8,16,4,128]{3,1,0,2:T(8,128)(2,1)} copy(bf16[8,16,4,128]{3,2,1,0:T(4,128)(2,1)} %param.7) | data formatting | bytes 262144 | tf_op args[0]
  2.4 0.8 broadcast_in_dim.2.mask
  3.2 84.6 %shard_map.73 = bf16[4,8,16,128]{3,2,1,0:T(8,128)(2,1)} custom-call(s32[2,3]{1,0:T(2,128)} %dilation.1, bf16[4,8,16,128]{3,2,1,0:T(8,128)(2,1)} %bitcast.8, f32[512,128]{1,0:T(8,128)} %broadcast_in_dim.2.mask, bf16[2,3456,128]{2,1,0:T(8,128)(2,1)} %conv_hbm.1, bf16[512,1024]{1,0:T(8,128)(2,1)} %bitcast.7, bf16[3,128,256]{2,1,0:T(8,128)(2,1)} %qkv_hbm.1, ...), custom_call_target="tpu_custom_call" | custom-call | tf_op jit(solution)/shard_map/pallas_call | solution.py:589
  87.8 1.7 %copy.12 = bf16[8,16,4,128]{3,2,1,0:T(4,128)(2,1)} copy(bf16[8,16,4,128]{3,1,0,2:T(8,128)(2,1)} %bitcast.9) | data formatting | bytes 262144 | tf_op jit(solution)/shard_map/transpose | solution.py:637
  (1 shorter events, 0.0 us)
